TPU v7x, 256 devices: a whole 4x4x8 slice. The times are simulated.
256 devices in a mesh: dp: 32 (over y, z), cent: 8 (over x, core).
Axes of the slice: x: 4, y: 4, z: 8, core: 2. Of those that a mesh axis runs over, the one named last changes fastest.
Arguments:
- stream: bfloat16 [65536, 768], P('dp'), may hold values from -6 to 6
- sample_index: int32 [32768], P('dp'), may hold values from 0 to 2047
- centroids: float32 [16384, 768], P(('cent', 'dp')), may hold values from -6 to 6
- first_moment: float32 [16384, 768], P(('cent', 'dp')), may hold values from -3 to 3
- second_moment: float32 [16384, 768], P(('cent', 'dp')), may hold values from 0.01 to 1
Outputs:
- new_centroids: float32 [16384, 768], P(('cent', 'dp'))
- new_first: float32 [16384, 768], P(('cent', 'dp'))
- new_second: float32 [16384, 768], P(('cent', 'dp'))
All inputs are finite; a program needn't handle non-finite values.
Results may differ from a plain program's by a relative error of at most 0.0003.
Values may be sent and summed in bfloat16 or wider, within the bound.
A program may use at most 64 MiB of HBM per device.

v0:
```python
import math
import jax
import jax.numpy as jnp
from jax import lax
from jax.sharding import PartitionSpec as P

KB = 16384
ITERS = 3
temper = 2.0
beta_one = 0.9
beta_two = 0.99
step_rate = 0.05
epsilon = 1e-08


def per_device(stream, sample_index, centroids, first_moment, second_moment):
    embedded = stream[sample_index]
    local_rows = embedded.shape[0]
    total_rows = local_rows * lax.axis_size("dp")
    balance = math.log(total_rows / KB)
    rounded = centroids.astype(jnp.bfloat16)
    shard_piece = lax.all_gather(rounded, "dp", axis=0, tiled=True)
    squares = jnp.sum(shard_piece.astype(jnp.float32) ** 2, axis=1)
    product = lax.dot_general(
        embedded, shard_piece, (((1,), (1,)), ((), ())), preferred_element_type=jnp.float32
    )
    logits = (2.0 * product - squares[None, :]) / temper

    def row_potential(column_pot):
        shifted = logits + column_pot[None, :]
        highest = jnp.max(shifted, axis=1)
        summed = jnp.sum(jnp.exp(shifted - highest[:, None]), axis=1)
        overall = lax.pmax(highest, "cent")
        summed = lax.psum(summed * jnp.exp(highest - overall), "cent")
        highest = overall
        return -(highest + jnp.log(summed))

    column_pot = jnp.zeros((logits.shape[1],), jnp.float32)
    for sweep_index in range(ITERS):
        column_shifted = logits + row_potential(column_pot)[:, None]
        column_highest = jnp.max(column_shifted, axis=0)
        column_summed = jnp.sum(jnp.exp(column_shifted - column_highest[None, :]), axis=0)
        column_overall = lax.pmax(column_highest, "dp")
        column_summed = lax.psum(column_summed * jnp.exp(column_highest - column_overall), "dp")
        column_highest = column_overall
        column_pot = balance - (column_highest + jnp.log(column_summed))
    row_pot = row_potential(column_pot)
    transport = jnp.exp(logits + row_pot[:, None] + column_pot[None, :]).astype(jnp.bfloat16)
    weighted = lax.dot_general(
        transport, embedded, (((0,), (0,)), ((), ())), preferred_element_type=jnp.float32
    )
    weight_mass = jnp.sum(transport.astype(jnp.float32), axis=0)
    weighted, weight_mass = lax.psum((weighted, weight_mass), "dp")
    owned_rows = centroids.shape[0]
    offset_rows = lax.axis_index("dp") * owned_rows
    weighted = lax.dynamic_slice_in_dim(weighted, offset_rows, owned_rows, 0)
    weight_mass = lax.dynamic_slice_in_dim(weight_mass, offset_rows, owned_rows, 0)
    gradient = (weight_mass[:, None] * centroids - weighted) * (KB / total_rows)
    new_first = beta_one * first_moment + (1.0 - beta_one) * gradient
    new_second = beta_two * second_moment + (1.0 - beta_two) * gradient * gradient
    new_centroids = centroids - step_rate * new_first / (jnp.sqrt(new_second) + epsilon)
    return (new_centroids, new_first, new_second)


def solution(mesh):
    return jax.shard_map(
        per_device,
        mesh=mesh,
        in_specs=(
            P("dp", None),
            P("dp"),
            P(("cent", "dp"), None),
            P(("cent", "dp"), None),
            P(("cent", "dp"), None),
        ),
        out_specs=(P(("cent", "dp"), None), P(("cent", "dp"), None), P(("cent", "dp"), None)),
        check_vma=False,
    )
```

profile of v0, /device:TPU:1, one launch (start us, length us, event | category | flops | bytes accessed | tf_op | source)
XLA Modules:
  0.0 889.1 jit_solution(12046903474257052355)
XLA Ops:
  7.2 0.0 copy-start
  7.2 0.0 all-gather.2.cloned.1.call-start
  7.2 1.7 convert_element_type.12
  9.0 0.0 all-gather.2.cloned.1.call-update
  9.0 0.0 all-reduce.2.cloned.1.call-start
  9.0 0.7 fusion
  9.7 0.0 copy-done
  9.7 5.2 gather_fusion
  15.0 76.0 %all-gather.2.cloned.1.call-done = bf16[2048,768]{1,0:T(8,128)(2,1)} async-done(((bf16[64,768]{1,0:T(8,128)(2,1)}), bf16[2048,768]{1,0:T(8,128)(2,1)}) %all-gather.2.cloned.1.call-update) | async-done | bytes 3145744 | tf_op jit(solution)/shard_map/all_gather | solution.py:22
  91.0 2.6 multiply_reduce_fusion
  93.6 9.1 %fusion.2 = (f32[1024]{0:T(1024)S(1)}, f32[1024,2048]{1,0:T(8,128)}) fusion(f32[2048]{0:T(1024)S(1)} %multiply_reduce_fusion, bf16[1024,768]{1,0:T(8,128)(2,1)} %gather_fusion, bf16[2048,768]{1,0:T(8,128)(2,1)} %all-gather.2.cloned.1.call-done), kind=kOutput, calls=%fused_computation.39 | convolution fusion | flops 3229613056 | bytes 13119488 | tf_op jit(solution)/shard_map/dot_general | solution.py:24
  102.6 16.4 %pmax.49 = f32[1024]{0:T(1024)S(1)} all-reduce(f32[1024]{0:T(1024)S(1)} %get-tuple-element.6), channel_id=1, replica_groups=mesh['dp'=32,'cent'=8] {'cent'}, use_global_device_ids=true, to_apply=%region_2.0 | all-reduce | flops 1024 | bytes 8192 | tf_op jit(solution)/shard_map/pmax | solution.py:33
  119.0 4.6 exponential_reduce_fusion.6
  123.6 12.4 %psum.63 = f32[1024]{0:T(1024)S(1)} all-reduce(f32[1024]{0:T(1024)S(1)} %exponential_multiply_fusion.6), channel_id=1, replica_groups=mesh['dp'=32,'cent'=8] {'cent'}, use_global_device_ids=true, to_apply=%region_4.0 | all-reduce | flops 1024 | bytes 8192 | tf_op jit(solution)/shard_map/psum | solution.py:34
  136.1 4.0 add_reduce_fusion.5
  140.1 4.3 exponential_reduce_fusion.5
  144.4 58.9 %pmax.50 = f32[2048]{0:T(1024)S(1)} all-reduce(f32[2048]{0:T(1024)S(1)} %add_reduce_fusion.5), channel_id=1, replica_groups=mesh['dp'=32,'cent'=8] {'dp'}, use_global_device_ids=true, to_apply=%region_6.0 | all-reduce | flops 2048 | bytes 16384 | tf_op jit(solution)/shard_map/pmax | solution.py:43
  203.3 56.7 %psum.64 = f32[2048]{0:T(1024)S(1)} all-reduce(f32[2048]{0:T(1024)S(1)} %exponential_multiply_fusion.2), channel_id=1, replica_groups=mesh['dp'=32,'cent'=8] {'dp'}, use_global_device_ids=true, to_apply=%region_8.0 | all-reduce | flops 2048 | bytes 16384 | tf_op jit(solution)/shard_map/psum | solution.py:44
  260.1 4.0 add_reduce_fusion.4
  264.1 4.4 exponential_reduce_fusion.4
  268.5 40.3 %pmax.51 = f32[1024]{0:T(1024)S(1)} all-reduce(f32[1024]{0:T(1024)S(1)} %add_reduce_fusion.4), channel_id=1, replica_groups=mesh['dp'=32,'cent'=8] {'cent'}, use_global_device_ids=true, to_apply=%region_10.0 | all-reduce | flops 1024 | bytes 8192 | tf_op jit(solution)/shard_map/pmax | solution.py:33
  308.8 12.4 %psum.65 = f32[1024]{0:T(1024)S(1)} all-reduce(f32[1024]{0:T(1024)S(1)} %exponential_multiply_fusion.5), channel_id=1, replica_groups=mesh['dp'=32,'cent'=8] {'cent'}, use_global_device_ids=true, to_apply=%region_12.0 | all-reduce | flops 1024 | bytes 8192 | tf_op jit(solution)/shard_map/psum | solution.py:34
  321.2 4.0 add_reduce_fusion.3
  325.3 4.3 exponential_reduce_fusion.3
  329.6 59.1 %pmax.52 = f32[2048]{0:T(1024)S(1)} all-reduce(f32[2048]{0:T(1024)S(1)} %add_reduce_fusion.3), channel_id=1, replica_groups=mesh['dp'=32,'cent'=8] {'dp'}, use_global_device_ids=true, to_apply=%region_14.0 | all-reduce | flops 2048 | bytes 16384 | tf_op jit(solution)/shard_map/pmax | solution.py:43
  388.7 57.2 %psum.66 = f32[2048]{0:T(1024)S(1)} all-reduce(f32[2048]{0:T(1024)S(1)} %exponential_multiply_fusion.1), channel_id=1, replica_groups=mesh['dp'=32,'cent'=8] {'dp'}, use_global_device_ids=true, to_apply=%region_16.0 | all-reduce | flops 2048 | bytes 16384 | tf_op jit(solution)/shard_map/psum | solution.py:44
  446.0 4.0 add_reduce_fusion.2
  450.0 4.4 exponential_reduce_fusion.2
  454.4 39.6 %pmax.53 = f32[1024]{0:T(1024)S(1)} all-reduce(f32[1024]{0:T(1024)S(1)} %add_reduce_fusion.2), channel_id=1, replica_groups=mesh['dp'=32,'cent'=8] {'cent'}, use_global_device_ids=true, to_apply=%region_18.0 | all-reduce | flops 1024 | bytes 8192 | tf_op jit(solution)/shard_map/pmax | solution.py:33
  494.0 12.4 %psum.67 = f32[1024]{0:T(1024)S(1)} all-reduce(f32[1024]{0:T(1024)S(1)} %exponential_multiply_fusion.4), channel_id=1, replica_groups=mesh['dp'=32,'cent'=8] {'cent'}, use_global_device_ids=true, to_apply=%region_20.0 | all-reduce | flops 1024 | bytes 8192 | tf_op jit(solution)/shard_map/psum | solution.py:34
  506.4 4.0 add_reduce_fusion.1
  510.4 4.3 exponential_reduce_fusion.1
  514.7 59.2 %pmax.54 = f32[2048]{0:T(1024)S(1)} all-reduce(f32[2048]{0:T(1024)S(1)} %add_reduce_fusion.1), channel_id=1, replica_groups=mesh['dp'=32,'cent'=8] {'dp'}, use_global_device_ids=true, to_apply=%region_22.0 | all-reduce | flops 2048 | bytes 16384 | tf_op jit(solution)/shard_map/pmax | solution.py:43
  573.9 57.0 %psum.68 = f32[2048]{0:T(1024)S(1)} all-reduce(f32[2048]{0:T(1024)S(1)} %exponential_multiply_fusion), channel_id=1, replica_groups=mesh['dp'=32,'cent'=8] {'dp'}, use_global_device_ids=true, to_apply=%region_24.0 | all-reduce | flops 2048 | bytes 16384 | tf_op jit(solution)/shard_map/psum | solution.py:44
  631.0 4.0 add_reduce_fusion
  635.0 4.4 exponential_reduce_fusion
  639.4 39.6 %pmax.55 = f32[1024]{0:T(1024)S(1)} all-reduce(f32[1024]{0:T(1024)S(1)} %add_reduce_fusion), channel_id=1, replica_groups=mesh['dp'=32,'cent'=8] {'cent'}, use_global_device_ids=true, to_apply=%region_26.0 | all-reduce | flops 1024 | bytes 8192 | tf_op jit(solution)/shard_map/pmax | solution.py:33
  679.0 12.4 %psum.69 = f32[1024]{0:T(1024)S(1)} all-reduce(f32[1024]{0:T(1024)S(1)} %exponential_multiply_fusion.3), channel_id=1, replica_groups=mesh['dp'=32,'cent'=8] {'cent'}, use_global_device_ids=true, to_apply=%region_28.0 | all-reduce | flops 1024 | bytes 8192 | tf_op jit(solution)/shard_map/psum | solution.py:34
  691.4 0.0 copy-start.3
  691.4 0.6 copy-done.3
  692.0 10.4 %fusion.1 = f32[2048,768]{1,0:T(8,128)} fusion(bf16[1024,768]{1,0:T(8,128)(2,1)} %gather_fusion, f32[1024,2048]{1,0:T(8,128)} %get-tuple-element.7, f32[1024]{0:T(1024)S(1)} %add_negate_fusion, f32[2048]{0:T(1024)S(1)} %add_subtract_fusion), kind=kOutput, calls=%fused_computation.38 | convolution fusion | flops 3227516928 | bytes 16265216 | tf_op jit(solution)/shard_map/dot_general | solution.py:49
  702.4 0.0 copy-start.1
  702.4 0.0 copy-start.2
  702.4 0.0 all-reduce.2.cloned.1.call-update
  702.4 4.3 convert_reduce_fusion
  706.8 61.3 %psum.70 = f32[2048]{0:T(1024)S(1)} all-reduce(f32[2048]{0:T(1024)S(1)} %convert_reduce_fusion), channel_id=1, replica_groups=mesh['dp'=32,'cent'=8] {'dp'}, use_global_device_ids=true, to_apply=%region_30.0 | all-reduce | flops 2048 | bytes 16384 | tf_op jit(solution)/shard_map/psum | solution.py:53
  768.0 0.1 dynamic_slice.6
  768.1 112.1 %all-reduce.2.cloned.1.call-done = f32[2048,768]{1,0:T(8,128)} async-done(((f32[2048,768]{1,0:T(8,128)}), f32[2048,768]{1,0:T(8,128)}) %all-reduce.2.cloned.1.call-update) | async-done | bytes 6291472 | tf_op jit(solution)/shard_map/psum | solution.py:53
  880.2 0.0 copy-done.1
  880.2 0.0 copy-done.2
  880.2 2.0 divide_subtract_fusion
  (14 shorter events, 0.1 us)
Async XLA Ops:
  7.2 2.6 copy-start
  7.2 83.8 %all-gather.2.cloned.1.call-start = ((), (), s32[]{:S(2)}) async-start(), calls=%async_computation | async-start | bytes 3244032 | tf_op jit(solution)/shard_map/all_gather | solution.py:22
  9.0 871.3 %all-reduce.2.cloned.1.call-start = ((), (), s32[]{:S(2)}) async-start(), calls=%async_computation.1 | async-start | bytes 12582912 | tf_op jit(solution)/shard_map/psum | solution.py:53
  691.4 0.6 copy-start.3
  702.4 177.9 %copy-start.1 = (f32[64,768]{1,0:T(8,128)S(1)}, f32[64,768]{1,0:T(8,128)}, u32[]{:S(2)}) copy-start(f32[64,768]{1,0:T(8,128)} %param.7) | copy-start | bytes 589828
  702.4 177.9 %copy-start.2 = (f32[64,768]{1,0:T(8,128)S(1)}, f32[64,768]{1,0:T(8,128)}, u32[]{:S(2)}) copy-start(f32[64,768]{1,0:T(8,128)} %param.8) | copy-start | bytes 589828
Sparse Core Ops, SparseCore 0:
  11.2 79.7 all-gather.1
  702.5 177.6 all-reduce.1
where the time goes:
time: 890 us; the launch traced here: 889 us
  blocking collectives  595 us (67%)
  waiting for transfers between devices  188 us (21%)
  other arithmetic  66.1 us (7%)
  matrix products  19.4 us (2%)
  between operations  14.3 us (2%)
    pmax x3, blocking collectives, per_device(): column_overall = lax.pmax(column_highest, 'dp')  177 us
    psum x3, blocking collectives, per_device(): lax.psum(column_summed * jnp.exp(column_highest - column_overall), 'dp')  171 us
    pmax x4, blocking collectives, row_potential(): overall = lax.pmax(highest, 'cent')  136 us
    psum x1, waiting for transfers between devices, per_device(): weighted, weight_mass = lax.psum((weighted, weight_mass), 'dp')  112 us
    all_gather x1, waiting for transfers between devices, per_device(): shard_piece = lax.all_gather(rounded, 'dp', axis=0, tiled=True)  76 us
    psum x1, blocking collectives, per_device(): weighted, weight_mass = lax.psum((weighted, weight_mass), 'dp')  61.3 us
    psum x4, blocking collectives, row_potential(): summed = lax.psum(summed * jnp.exp(highest - overall), 'cent')  49.7 us
  transfers between devices with their start and end apart: 2, of which 2 were waited for; matrix products, arithmetic and copies ran while one was open for 1% of the time, Pallas kernels for 0%

commit v1 on v0

--- a/solution.py
+++ b/solution.py
@@ -19,7 +19,10 @@
     total_rows = local_rows * lax.axis_size("dp")
     balance = math.log(total_rows / KB)
     rounded = centroids.astype(jnp.bfloat16)
-    shard_piece = lax.all_gather(rounded, "dp", axis=0, tiled=True)
+    size = lax.axis_size("dp")
+    tiles = jnp.stack([rounded for _ in range(size)])
+    tiles = lax.all_to_all(tiles, "dp", split_axis=0, concat_axis=0)
+    shard_piece = jnp.concatenate(tiles, axis=0)
     squares = jnp.sum(shard_piece.astype(jnp.float32) ** 2, axis=1)
     product = lax.dot_general(
         embedded, shard_piece, (((1,), (1,)), ((), ())), preferred_element_type=jnp.float32

time: 890 us -> 893 us (level)
  starting transfers between devices: 0.08 us -> 12.2 us
  waiting for transfers between devices: 188 us -> 178 us
    all_gather x1 -> x0, waiting for transfers between devices: 76 us -> none  [per_device(): shard_piece = lax.all_gather(rounded, 'dp', axis=0, tiled=True)]
    all_to_all x0 -> x1, waiting for transfers between devices: none -> 66.2 us  [per_device(): tiles = lax.all_to_all(tiles, 'dp', split_axis=0, concat_axis=0)]
    all_to_all x0 -> x1, starting transfers between devices: none -> 12.1 us  [per_device(): tiles = lax.all_to_all(tiles, 'dp', split_axis=0, concat_axis=0)]
where the time goes in v1:
time: 893 us; the launch traced here: 892 us
  blocking collectives  595 us (67%)
  waiting for transfers between devices  178 us (20%)
  other arithmetic  64.8 us (7%)
  matrix products  19.4 us (2%)
  between operations  14.3 us (2%)
  starting transfers between devices  12.2 us (1%)
    pmax x3, blocking collectives, per_device(): column_overall = lax.pmax(column_highest, 'dp')  177 us
    psum x3, blocking collectives, per_device(): lax.psum(column_summed * jnp.exp(column_highest - column_overall), 'dp')  171 us
    pmax x4, blocking collectives, row_potential(): overall = lax.pmax(highest, 'cent')  136 us
    psum x1, waiting for transfers between devices, per_device(): weighted, weight_mass = lax.psum((weighted, weight_mass), 'dp')  112 us
    all_to_all x1, waiting for transfers between devices, per_device(): tiles = lax.all_to_all(tiles, 'dp', split_axis=0, concat_axis=0)  66.2 us
    psum x1, blocking collectives, per_device(): weighted, weight_mass = lax.psum((weighted, weight_mass), 'dp')  61.2 us
    psum x4, blocking collectives, row_potential(): summed = lax.psum(summed * jnp.exp(highest - overall), 'cent')  49.7 us
  transfers between devices with their start and end apart: 2, of which 2 were waited for; matrix products, arithmetic and copies ran while one was open for 1% of the time, Pallas kernels for 0%

profile of v1, /device:TPU:1, one launch (start us, length us, event | category | flops | bytes accessed | tf_op | source)
XLA Modules:
  0.0 892.0 jit_solution(1177248562189263842)
XLA Ops:
  7.2 0.0 copy-start
  7.2 0.0 copy-start.4
  7.2 1.1 convert_element_type.13
  8.3 2.0 stack.2
  10.3 12.1 %all-to-all-start = ((bf16[32,64,768]{2,1,0:T(8,128)(2,1)}), bf16[32,64,768]{2,1,0:T(8,128)(2,1)}, u32[]{:S(2)}, u32[]{:S(2)}) async-start(bf16[32,64,768]{2,1,0:T(8,128)(2,1)} %stack.2), calls=%async_computation | async-start | bytes 6291456 | tf_op jit(solution)/shard_map/all_to_all | solution.py:24
  22.5 0.0 all-reduce.2.cloned.1.call-start
  22.5 0.0 copy-done.4
  22.5 0.0 copy-done
  22.6 5.2 gather_fusion
  27.8 66.2 %all-to-all-done = bf16[32,64,768]{2,1,0:T(8,128)(2,1)} async-done(((bf16[32,64,768]{2,1,0:T(8,128)(2,1)}), bf16[32,64,768]{2,1,0:T(8,128)(2,1)}, u32[]{:S(2)}, u32[]{:S(2)}) %all-to-all-start) | async-done | bytes 3145760 | tf_op jit(solution)/shard_map/all_to_all | solution.py:24
  94.0 2.6 multiply_reduce_fusion
  96.5 0.1 sub.102
  96.6 9.1 %fusion.2 = (f32[1024]{0:T(1024)S(1)}, f32[1024,2048]{1,0:T(8,128)}) fusion(f32[2048]{0:T(1024)S(1)} %sub.102, bf16[1024,768]{1,0:T(8,128)(2,1)} %gather_fusion, bf16[2048,768]{1,0:T(8,128)(2,1)} %bitcast), kind=kOutput, calls=%fused_computation.39 | convolution fusion | flops 3229613056 | bytes 13119488 | tf_op jit(solution)/shard_map/dot_general | solution.py:27
  105.7 15.9 %pmax.49 = f32[1024]{0:T(1024)S(1)} all-reduce(f32[1024]{0:T(1024)S(1)} %get-tuple-element.6), channel_id=1, replica_groups=mesh['dp'=32,'cent'=8] {'cent'}, use_global_device_ids=true, to_apply=%region_2.0 | all-reduce | flops 1024 | bytes 8192 | tf_op jit(solution)/shard_map/pmax | solution.py:36
  121.5 4.6 exponential_reduce_fusion.6
  126.2 12.4 %psum.63 = f32[1024]{0:T(1024)S(1)} all-reduce(f32[1024]{0:T(1024)S(1)} %exponential_multiply_fusion.6), channel_id=1, replica_groups=mesh['dp'=32,'cent'=8] {'cent'}, use_global_device_ids=true, to_apply=%region_4.0 | all-reduce | flops 1024 | bytes 8192 | tf_op jit(solution)/shard_map/psum | solution.py:37
  138.6 4.0 add_reduce_fusion.5
  142.6 4.3 exponential_reduce_fusion.5
  146.9 59.0 %pmax.50 = f32[2048]{0:T(1024)S(1)} all-reduce(f32[2048]{0:T(1024)S(1)} %add_reduce_fusion.5), channel_id=1, replica_groups=mesh['dp'=32,'cent'=8] {'dp'}, use_global_device_ids=true, to_apply=%region_6.0 | all-reduce | flops 2048 | bytes 16384 | tf_op jit(solution)/shard_map/pmax | solution.py:46
  206.0 56.8 %psum.64 = f32[2048]{0:T(1024)S(1)} all-reduce(f32[2048]{0:T(1024)S(1)} %exponential_multiply_fusion.2), channel_id=1, replica_groups=mesh['dp'=32,'cent'=8] {'dp'}, use_global_device_ids=true, to_apply=%region_8.0 | all-reduce | flops 2048 | bytes 16384 | tf_op jit(solution)/shard_map/psum | solution.py:47
  262.8 4.0 add_reduce_fusion.4
  266.8 4.4 exponential_reduce_fusion.4
  271.2 40.5 %pmax.51 = f32[1024]{0:T(1024)S(1)} all-reduce(f32[1024]{0:T(1024)S(1)} %add_reduce_fusion.4), channel_id=1, replica_groups=mesh['dp'=32,'cent'=8] {'cent'}, use_global_device_ids=true, to_apply=%region_10.0 | all-reduce | flops 1024 | bytes 8192 | tf_op jit(solution)/shard_map/pmax | solution.py:36
  311.7 12.4 %psum.65 = f32[1024]{0:T(1024)S(1)} all-reduce(f32[1024]{0:T(1024)S(1)} %exponential_multiply_fusion.5), channel_id=1, replica_groups=mesh['dp'=32,'cent'=8] {'cent'}, use_global_device_ids=true, to_apply=%region_12.0 | all-reduce | flops 1024 | bytes 8192 | tf_op jit(solution)/shard_map/psum | solution.py:37
  324.1 4.0 add_reduce_fusion.3
  328.1 4.3 exponential_reduce_fusion.3
  332.4 59.1 %pmax.52 = f32[2048]{0:T(1024)S(1)} all-reduce(f32[2048]{0:T(1024)S(1)} %add_reduce_fusion.3), channel_id=1, replica_groups=mesh['dp'=32,'cent'=8] {'dp'}, use_global_device_ids=true, to_apply=%region_14.0 | all-reduce | flops 2048 | bytes 16384 | tf_op jit(solution)/shard_map/pmax | solution.py:46
  391.6 57.2 %psum.66 = f32[2048]{0:T(1024)S(1)} all-reduce(f32[2048]{0:T(1024)S(1)} %exponential_multiply_fusion.1), channel_id=1, replica_groups=mesh['dp'=32,'cent'=8] {'dp'}, use_global_device_ids=true, to_apply=%region_16.0 | all-reduce | flops 2048 | bytes 16384 | tf_op jit(solution)/shard_map/psum | solution.py:47
  448.9 4.0 add_reduce_fusion.2
  452.9 4.4 exponential_reduce_fusion.2
  457.3 39.6 %pmax.53 = f32[1024]{0:T(1024)S(1)} all-reduce(f32[1024]{0:T(1024)S(1)} %add_reduce_fusion.2), channel_id=1, replica_groups=mesh['dp'=32,'cent'=8] {'cent'}, use_global_device_ids=true, to_apply=%region_18.0 | all-reduce | flops 1024 | bytes 8192 | tf_op jit(solution)/shard_map/pmax | solution.py:36
  496.9 12.4 %psum.67 = f32[1024]{0:T(1024)S(1)} all-reduce(f32[1024]{0:T(1024)S(1)} %exponential_multiply_fusion.4), channel_id=1, replica_groups=mesh['dp'=32,'cent'=8] {'cent'}, use_global_device_ids=true, to_apply=%region_20.0 | all-reduce | flops 1024 | bytes 8192 | tf_op jit(solution)/shard_map/psum | solution.py:37
  509.3 4.0 add_reduce_fusion.1
  513.3 4.3 exponential_reduce_fusion.1
  517.6 59.2 %pmax.54 = f32[2048]{0:T(1024)S(1)} all-reduce(f32[2048]{0:T(1024)S(1)} %add_reduce_fusion.1), channel_id=1, replica_groups=mesh['dp'=32,'cent'=8] {'dp'}, use_global_device_ids=true, to_apply=%region_22.0 | all-reduce | flops 2048 | bytes 16384 | tf_op jit(solution)/shard_map/pmax | solution.py:46
  576.8 57.0 %psum.68 = f32[2048]{0:T(1024)S(1)} all-reduce(f32[2048]{0:T(1024)S(1)} %exponential_multiply_fusion), channel_id=1, replica_groups=mesh['dp'=32,'cent'=8] {'dp'}, use_global_device_ids=true, to_apply=%region_24.0 | all-reduce | flops 2048 | bytes 16384 | tf_op jit(solution)/shard_map/psum | solution.py:47
  633.9 4.0 add_reduce_fusion
  637.9 4.4 exponential_reduce_fusion
  642.3 39.6 %pmax.55 = f32[1024]{0:T(1024)S(1)} all-reduce(f32[1024]{0:T(1024)S(1)} %add_reduce_fusion), channel_id=1, replica_groups=mesh['dp'=32,'cent'=8] {'cent'}, use_global_device_ids=true, to_apply=%region_26.0 | all-reduce | flops 1024 | bytes 8192 | tf_op jit(solution)/shard_map/pmax | solution.py:36
  681.9 12.4 %psum.69 = f32[1024]{0:T(1024)S(1)} all-reduce(f32[1024]{0:T(1024)S(1)} %exponential_multiply_fusion.3), channel_id=1, replica_groups=mesh['dp'=32,'cent'=8] {'cent'}, use_global_device_ids=true, to_apply=%region_28.0 | all-reduce | flops 1024 | bytes 8192 | tf_op jit(solution)/shard_map/psum | solution.py:37
  694.3 0.0 copy-start.3
  694.3 0.6 copy-done.3
  694.9 10.4 %fusion.1 = f32[2048,768]{1,0:T(8,128)} fusion(bf16[1024,768]{1,0:T(8,128)(2,1)} %gather_fusion, f32[1024,2048]{1,0:T(8,128)} %get-tuple-element.7, f32[1024]{0:T(1024)S(1)} %add_negate_fusion, f32[2048]{0:T(1024)S(1)} %add_subtract_fusion), kind=kOutput, calls=%fused_computation.38 | convolution fusion | flops 3227516928 | bytes 16265216 | tf_op jit(solution)/shard_map/dot_general | solution.py:52
  705.3 0.0 copy-start.1
  705.3 0.0 copy-start.2
  705.3 0.0 all-reduce.2.cloned.1.call-update
  705.3 4.3 convert_reduce_fusion
  709.6 61.2 %psum.70 = f32[2048]{0:T(1024)S(1)} all-reduce(f32[2048]{0:T(1024)S(1)} %convert_reduce_fusion), channel_id=1, replica_groups=mesh['dp'=32,'cent'=8] {'dp'}, use_global_device_ids=true, to_apply=%region_30.0 | all-reduce | flops 2048 | bytes 16384 | tf_op jit(solution)/shard_map/psum | solution.py:56
  770.8 0.1 dynamic_slice.6
  770.9 112.2 %all-reduce.2.cloned.1.call-done = f32[2048,768]{1,0:T(8,128)} async-done(((f32[2048,768]{1,0:T(8,128)}), f32[2048,768]{1,0:T(8,128)}) %all-reduce.2.cloned.1.call-update) | async-done | bytes 6291472 | tf_op jit(solution)/shard_map/psum | solution.py:56
  883.1 0.0 copy-done.1
  883.2 0.0 copy-done.2
  883.2 2.0 divide_subtract_fusion
  (15 shorter events, 0.1 us)
Async XLA Ops:
  7.2 15.4 %copy-start = (bf16[2048,768]{1,0:T(8,128)(2,1)S(1)}, bf16[2048,768]{1,0:T(8,128)(2,1)}, u32[]{:S(2)}) copy-start(bf16[2048,768]{1,0:T(8,128)(2,1)} %param.5) | copy-start | bytes 9437188
  7.2 15.3 %copy-start.4 = (s32[1024]{0:T(1024)S(1)}, s32[1024]{0:T(1024)}, u32[]{:S(2)}) copy-start(s32[1024]{0:T(1024)} %param.6) | copy-start | bytes 12292
  10.3 83.7 %all-to-all-start = ((bf16[32,64,768]{2,1,0:T(8,128)(2,1)}), bf16[32,64,768]{2,1,0:T(8,128)(2,1)}, u32[]{:S(2)}, u32[]{:S(2)}) async-start(bf16[32,64,768]{2,1,0:T(8,128)(2,1)} %stack.2), calls=%async_computation | async-start | bytes 6291456 | tf_op jit(solution)/shard_map/all_to_all | solution.py:24
  22.5 860.7 %all-reduce.2.cloned.1.call-start = ((), (), s32[]{:S(2)}) async-start(), calls=%async_computation.1 | async-start | bytes 12582912 | tf_op jit(solution)/shard_map/psum | solution.py:56
  694.3 0.6 copy-start.3
  705.3 177.9 %copy-start.1 = (f32[64,768]{1,0:T(8,128)S(1)}, f32[64,768]{1,0:T(8,128)}, u32[]{:S(2)}) copy-start(f32[64,768]{1,0:T(8,128)} %param.7) | copy-start | bytes 589828
  705.3 177.9 %copy-start.2 = (f32[64,768]{1,0:T(8,128)S(1)}, f32[64,768]{1,0:T(8,128)}, u32[]{:S(2)}) copy-start(f32[64,768]{1,0:T(8,128)} %param.8) | copy-start | bytes 589828
Sparse Core Ops, SparseCore 0:
  705.4 177.7 all-reduce.1
